TPU v7x, 128 devices: a whole 4x4x4 slice. The times are simulated.
128 devices in a mesh: row: 8 (over x, y_hi), col: 16 (over y_lo, z, core).
Axes of the slice: x: 4, y: 4 (y_hi: 2, y_lo: 2; y = y_hi * 2 + y_lo), z: 4, core: 2. Of those that a mesh axis runs over, the one named last changes fastest.
Arguments:
- coupling: bfloat16 [32768, 32768], P('row', 'col'), may hold values from -0.03125 to 0.03125
- amplitude: float32 [64, 32768], P(None, 'col'), may hold values from -0.95 to 0.95
- target: float32 [64, 32768], P(None, 'col'), may hold values from -6 to 6
- shadow_target: float32 [64, 32768], P(None, 'col'), may hold values from -10.2 to 10.2
Outputs:
- solution: float32 [64, 32768], P(None, 'col')
- shadow_solution: float32 [64, 32768], P(None, 'col')
- residual: float32 [64, 32768], P(None, 'col')
- shadow_residual: float32 [64, 32768], P(None, 'col')
All inputs are finite; a program needn't handle non-finite values.
Results may differ from a plain program's by a relative error of at most 0.0036.
Values may be sent and summed in bfloat16 or wider, within the bound.
No kernel may reach another device: no remote copies, remote signals or barrier semaphores. Data moves between devices by JAX's collectives and lax.ppermute only.
A program may use at most 128 MiB of HBM per device.

v0:
```python
import jax
import jax.numpy as jnp
from jax import lax
from jax.sharding import PartitionSpec as P

ITERS = 2
SELF_GAIN = 0.5
COUPLE_GAIN = 0.3


def on_device(coupling, amplitude, target, shadow_target):
    row_rows = coupling.shape[0]
    col_rows = coupling.shape[1]
    row_index = lax.axis_index("row")
    col_index = lax.axis_index("col")
    slope = 1.0 - amplitude * amplitude
    solution = jnp.zeros_like(target)
    shadow_solution = jnp.zeros_like(target)
    residual = target
    shadow_residual = shadow_target
    direction = target
    shadow_direction = shadow_target
    align = lax.psum(jnp.sum(shadow_residual * residual, axis=1), "col")
    for iteration in range(ITERS):
        scaled = (slope * direction).astype(jnp.bfloat16)
        primary_gathered = lax.all_gather(scaled, "col", axis=1, tiled=True)
        row_block = lax.dynamic_slice_in_dim(primary_gathered, row_index * row_rows, row_rows, 1)
        primary_partial_value = jnp.dot(row_block, coupling, preferred_element_type=jnp.float32)
        product = lax.psum(primary_partial_value, "row")
        image = direction - SELF_GAIN * slope * direction - COUPLE_GAIN * product
        shadow_scaled = shadow_direction.astype(jnp.bfloat16)
        partial_value = lax.dot_general(
            shadow_scaled, coupling, (((1,), (1,)), ((), ())), preferred_element_type=jnp.float32
        )
        summed = lax.psum(partial_value, "col")
        gathered = lax.all_gather(summed, "row", axis=1, tiled=True)
        own_block = lax.dynamic_slice_in_dim(gathered, col_index * col_rows, col_rows, 1)
        shadow_image = (
            shadow_direction
            - SELF_GAIN * slope * shadow_direction
            - COUPLE_GAIN * slope * own_block
        )
        curve = lax.psum(jnp.sum(shadow_direction * image, axis=1), "col")
        step_size = align / curve
        column_step = step_size[:, None]
        solution = solution + column_step * direction
        shadow_solution = shadow_solution + column_step * shadow_direction
        residual = residual - column_step * image
        shadow_residual = shadow_residual - column_step * shadow_image
        if iteration + 1 < ITERS:
            align_next = lax.psum(jnp.sum(shadow_residual * residual, axis=1), "col")
        if iteration + 1 < ITERS:
            blend = (align_next / align)[:, None]
            direction = residual + blend * direction
            shadow_direction = shadow_residual + blend * shadow_direction
            align = align_next
    return (solution, shadow_solution, residual, shadow_residual)


def solution(mesh):
    return jax.shard_map(
        on_device,
        mesh=mesh,
        in_specs=(P("row", "col"), P(None, "col"), P(None, "col"), P(None, "col")),
        out_specs=(P(None, "col"), P(None, "col"), P(None, "col"), P(None, "col")),
        check_vma=False,
    )
```

profile of v0, /device:TPU:1, one launch (start us, length us, event | category | flops | bytes accessed | tf_op | source)
XLA Modules:
  0.0 766.5 jit_solution(14258358741011477803)
XLA Ops:
  7.2 2.1 multiply_convert_fusion.1
  9.4 12.1 %fusion.14 = f32[64,4096]{1,0:T(8,128)} fusion(bf16[4096,2048]{1,0:T(8,128)(2,1)} %param.4, f32[64,2048]{1,0:T(8,128)} %param.7), kind=kOutput, calls=%fused_computation.31 | convolution fusion | flops 1073872896 | bytes 18350080 | tf_op jit(solution)/shard_map/dot_general | solution.py:32
  21.6 29.8 %all-gather.5.cloned.1.call-done = bf16[64,32768]{1,0:T(8,128)(2,1)} async-done(((bf16[64,2048]{1,0:T(8,128)(2,1)}), bf16[64,32768]{1,0:T(8,128)(2,1)}) %all-gather.5.cloned.1.call-update) | async-done | bytes 4194320 | tf_op jit(solution)/shard_map/all_gather | solution.py:26
  51.3 9.8 %fusion.10 = f32[64,2048]{1,0:T(8,128)} fusion(bf16[4096,2048]{1,0:T(8,128)(2,1)} %param.4, bf16[64,32768]{1,0:T(8,128)(2,1)} %all-gather.5.cloned.1.call-done, s32[]{:T(128)S(6)} %select_n.8), kind=kOutput, calls=%fused_computation.24 | convolution fusion | flops 1073741824 | bytes 17825796 | tf_op jit(solution)/shard_map/dot_general | solution.py:28
  61.2 111.6 %all-reduce.8.cloned.1.call-done = f32[64,4096]{1,0:T(8,128)} async-done(((f32[64,4096]{1,0:T(8,128)}), f32[64,4096]{1,0:T(8,128)}) %all-reduce.8.cloned.1.call-update) | async-done | bytes 1048592 | tf_op jit(solution)/shard_map/psum | solution.py:35
  172.9 84.5 %all-reduce.6.cloned.1.call-done = f32[64,2048]{1,0:T(8,128)} async-done(((f32[64,2048]{1,0:T(8,128)}), f32[64,2048]{1,0:T(8,128)}) %all-reduce.6.cloned.1.call-update) | async-done | bytes 524304 | tf_op jit(solution)/shard_map/psum | solution.py:29
  257.3 1.3 multiply_reduce_fusion.2
  258.7 32.6 %all-reduce = (f32[64]{0:T(128)S(1)}, f32[64]{0:T(128)S(1)}) all-reduce(f32[64]{0:T(128)S(1)} %get-tuple-element.5, f32[64]{0:T(128)S(1)} %get-tuple-element.4), channel_id=1, replica_groups=mesh['row'=8,'col'=16] {'col'}, use_global_device_ids=true, to_apply=%region_1.0 | all-reduce | flops 128 | bytes 1024 | tf_op jit(solution)/shard_map/psum | solution.py:23
  291.3 79.8 %all-gather.7.cloned.1.call-done = f32[64,32768]{1,0:T(8,128)} async-done(((f32[64,4096]{1,0:T(8,128)}), f32[64,32768]{1,0:T(8,128)}) %all-gather.7.cloned.1.call-update) | async-done | bytes 8388624 | tf_op jit(solution)/shard_map/all_gather | solution.py:36
  371.0 1.6 multiply_reduce_fusion.1
  372.7 27.6 %psum.60 = f32[64]{0:T(128)S(1)} all-reduce(f32[64]{0:T(128)S(1)} %get-tuple-element.10), channel_id=1, replica_groups=mesh['row'=8,'col'=16] {'col'}, use_global_device_ids=true, to_apply=%region_7.0 | all-reduce | flops 64 | bytes 512 | tf_op jit(solution)/shard_map/psum | solution.py:51
  400.3 0.9 multiply_convert_fusion
  401.1 0.0 all-reduce.12.cloned.1.call-start
  401.2 12.0 %fusion.12 = f32[64,4096]{1,0:T(8,128)} fusion(bf16[4096,2048]{1,0:T(8,128)(2,1)} %param.4, f32[64,2048]{1,0:T(8,128)S(1)} %get-tuple-element.12, f32[64,2048]{1,0:T(8,128)S(1)} %copy-done, f32[64]{0:T(128)S(1)} %div.10), kind=kOutput, calls=%fused_computation.29 | convolution fusion | flops 1074135040 | bytes 18874624 | tf_op jit(solution)/shard_map/dot_general | solution.py:32
  413.2 0.2 all-reduce.10.cloned.1.call-start
  413.4 23.9 %all-gather.9.cloned.1.call-done = bf16[64,32768]{1,0:T(8,128)(2,1)} async-done(((bf16[64,2048]{1,0:T(8,128)(2,1)}), bf16[64,32768]{1,0:T(8,128)(2,1)}) %all-gather.9.cloned.1.call-update) | async-done | bytes 4194320 | tf_op jit(solution)/shard_map/all_gather | solution.py:26
  437.4 9.8 %fusion.8 = f32[64,2048]{1,0:T(8,128)} fusion(bf16[4096,2048]{1,0:T(8,128)(2,1)} %param.4, bf16[64,32768]{1,0:T(8,128)(2,1)} %all-gather.9.cloned.1.call-done, s32[]{:T(128)S(6)} %select_n.8), kind=kOutput, calls=%fused_computation.16 | convolution fusion | flops 1073741824 | bytes 17825796 | tf_op jit(solution)/shard_map/dot_general | solution.py:28
  447.1 0.0 all-gather.11.cloned.1.call-start
  447.2 111.4 %all-reduce.12.cloned.1.call-done = f32[64,4096]{1,0:T(8,128)} async-done(((f32[64,4096]{1,0:T(8,128)}), f32[64,4096]{1,0:T(8,128)}) %all-reduce.12.cloned.1.call-update) | async-done | bytes 1048592 | tf_op jit(solution)/shard_map/psum | solution.py:35
  558.7 84.5 %all-reduce.10.cloned.1.call-done = f32[64,2048]{1,0:T(8,128)} async-done(((f32[64,2048]{1,0:T(8,128)}), f32[64,2048]{1,0:T(8,128)}) %all-reduce.10.cloned.1.call-update) | async-done | bytes 524304 | tf_op jit(solution)/shard_map/psum | solution.py:29
  643.2 1.4 multiply_reduce_fusion
  644.6 32.6 %psum.62 = f32[64]{0:T(128)S(1)} all-reduce(f32[64]{0:T(128)S(1)} %get-tuple-element.8), channel_id=1, replica_groups=mesh['row'=8,'col'=16] {'col'}, use_global_device_ids=true, to_apply=%region_10.0 | all-reduce | flops 64 | bytes 512 | tf_op jit(solution)/shard_map/psum | solution.py:43
  677.2 79.8 %all-gather.11.cloned.1.call-done = f32[64,32768]{1,0:T(8,128)} async-done(((f32[64,4096]{1,0:T(8,128)}), f32[64,32768]{1,0:T(8,128)}) %all-gather.11.cloned.1.call-update) | async-done | bytes 8388624 | tf_op jit(solution)/shard_map/all_gather | solution.py:36
  757.0 2.7 multiply_subtract_fusion.4
  (22 shorter events, 0.4 us)
Async XLA Ops:
  7.2 44.2 %all-gather.5.cloned.1.call-start = ((), (), s32[]{:S(2)}) async-start(), calls=%async_computation | async-start | bytes 4456448 | tf_op jit(solution)/shard_map/all_gather | solution.py:26
  9.3 163.5 %all-reduce.8.cloned.1.call-start = ((), (), s32[]{:S(2)}) async-start(), calls=%async_computation.2 | async-start | bytes 2097152 | tf_op jit(solution)/shard_map/psum | solution.py:35
  21.5 235.8 %copy-start = (f32[64,2048]{1,0:T(8,128)S(1)}, f32[64,2048]{1,0:T(8,128)}, u32[]{:S(2)}) copy-start(f32[64,2048]{1,0:T(8,128)} %param.7) | copy-start | bytes 1572868
  21.5 235.8 %copy-start.1 = (f32[64,2048]{1,0:T(8,128)S(1)}, f32[64,2048]{1,0:T(8,128)}, u32[]{:S(2)}) copy-start(f32[64,2048]{1,0:T(8,128)} %param.6) | copy-start | bytes 1572868
  21.5 235.8 %copy-start.2 = (f32[64,2048]{1,0:T(8,128)S(1)}, f32[64,2048]{1,0:T(8,128)}, u32[]{:S(2)}) copy-start(f32[64,2048]{1,0:T(8,128)} %param.5) | copy-start | bytes 1572868
  21.5 235.8 %all-reduce.6.cloned.1.call-start = ((), (), s32[]{:S(2)}) async-start(), calls=%async_computation.1 | async-start | bytes 1048576 | tf_op jit(solution)/shard_map/psum | solution.py:29
  61.1 309.9 %all-gather.7.cloned.1.call-start = ((), (), s32[]{:S(2)}) async-start(), calls=%async_computation.3 | async-start | bytes 9437184 | tf_op jit(solution)/shard_map/all_gather | solution.py:36
  172.8 264.5 %all-gather.9.cloned.1.call-start = ((), (), s32[]{:S(2)}) async-start(), calls=%async_computation.4 | async-start | bytes 4456448 | tf_op jit(solution)/shard_map/all_gather | solution.py:26
  401.1 157.5 %all-reduce.12.cloned.1.call-start = ((), (), s32[]{:S(2)}) async-start(), calls=%async_computation.6 | async-start | bytes 2097152 | tf_op jit(solution)/shard_map/psum | solution.py:35
  413.2 230.0 %all-reduce.10.cloned.1.call-start = ((), (), s32[]{:S(2)}) async-start(), calls=%async_computation.5 | async-start | bytes 1048576 | tf_op jit(solution)/shard_map/psum | solution.py:29
  447.1 309.9 %all-gather.11.cloned.1.call-start = ((), (), s32[]{:S(2)}) async-start(), calls=%async_computation.7 | async-start | bytes 9437184 | tf_op jit(solution)/shard_map/all_gather | solution.py:36
Sparse Core Ops, SparseCore 0:
  10.2 41.0 all-gather.4
  53.8 118.9 all-reduce.7
  176.0 81.2 all-reduce.5
  259.5 111.4 all-gather.6
  401.2 36.0 all-gather.8
  439.7 118.9 all-reduce.11
  561.9 81.2 all-reduce.9
  645.5 111.4 all-gather.10
where the time goes:
time: 767 us
  waiting for transfers between devices  605 us (79%)
  blocking collectives  92.8 us (12%)
  matrix products  43.6 us (6%)
  between operations  14.2 us (2%)
  other arithmetic  10 us (1%)
    psum x2, waiting for transfers between devices, on_device(): summed = lax.psum(partial_value, 'col')  223 us
    psum x2, waiting for transfers between devices, on_device(): product = lax.psum(primary_partial_value, 'row')  169 us
    all_gather x2, waiting for transfers between devices, on_device(): gathered = lax.all_gather(summed, 'row', axis=1, tiled=True)  160 us
    all_gather x2, waiting for transfers between devices, on_device(): primary_gathered = lax.all_gather(scaled, 'col', axis=1, tiled=True)  53.7 us
    psum x1, blocking collectives, on_device(): curve = lax.psum(jnp.sum(shadow_direction * image, axis=1), 'col')  32.6 us
    psum x1, blocking collectives, on_device(): align = lax.psum(jnp.sum(shadow_residual * residual, axis=1), 'col')  32.6 us
    psum x1, blocking collectives, on_device(): align_next = lax.psum(jnp.sum(shadow_residual * residual, axis=1), 'col')  27.6 us
    dot_general x2, matrix products, on_device(): lax.dot_general(shadow_scaled, coupling, (((1,), (1,)), ((), ())), prefer...  24.1 us
  transfers between devices with their start and end apart: 8, of which 8 were waited for; matrix products, arithmetic and copies ran while one was open for 6% of the time, Pallas kernels for 0%

commit v1 on v0

--- a/solution.py
+++ b/solution.py
@@ -26,7 +26,7 @@
         primary_gathered = lax.all_gather(scaled, "col", axis=1, tiled=True)
         row_block = lax.dynamic_slice_in_dim(primary_gathered, row_index * row_rows, row_rows, 1)
         primary_partial_value = jnp.dot(row_block, coupling, preferred_element_type=jnp.float32)
-        product = lax.psum(primary_partial_value, "row")
+        product = lax.all_gather(primary_partial_value, axis_name="row").sum(axis=0)
         image = direction - SELF_GAIN * slope * direction - COUPLE_GAIN * product
         shadow_scaled = shadow_direction.astype(jnp.bfloat16)
         partial_value = lax.dot_general(

time: 767 us -> 739 us (0.963)
  waiting for transfers between devices: 605 us -> 584 us
  blocking collectives: 92.8 us -> 83 us
    psum x2 -> x0, waiting for transfers between devices: 169 us -> none  [on_device(): product = lax.psum(primary_partial_value, 'row')]
    all_gather x0 -> x2, waiting for transfers between devices: none -> 150 us  [on_device(): product = lax.all_gather(primary_partial_value, axis_name='row').sum(axis=0)]
  transfers between devices with their start and end apart: 8 -> 8, of which waited for: 8 -> 8; matrix products, arithmetic and copies ran while one was open for 6% -> 7% of each run, Pallas kernels for 0% -> 0%
where the time goes in v1:
time: 739 us
  waiting for transfers between devices  584 us (79%)
  blocking collectives  83 us (11%)
  matrix products  43.6 us (6%)
  between operations  14.2 us (2%)
  other arithmetic  13.6 us (2%)
    psum x2, waiting for transfers between devices, on_device(): summed = lax.psum(partial_value, 'col')  223 us
    all_gather x2, waiting for transfers between devices, on_device(): gathered = lax.all_gather(summed, 'row', axis=1, tiled=True)  156 us
    all_gather x2, waiting for transfers between devices, on_device(): product = lax.all_gather(primary_partial_value, axis_name='row').sum(axis=0)  150 us
    all_gather x2, waiting for transfers between devices, on_device(): primary_gathered = lax.all_gather(scaled, 'col', axis=1, tiled=True)  53.8 us
    psum x1, blocking collectives, on_device(): curve = lax.psum(jnp.sum(shadow_direction * image, axis=1), 'col')  27.7 us
    psum x1, blocking collectives, on_device(): align = lax.psum(jnp.sum(shadow_residual * residual, axis=1), 'col')  27.7 us
    psum x1, blocking collectives, on_device(): align_next = lax.psum(jnp.sum(shadow_residual * residual, axis=1), 'col')  27.6 us
    dot_general x2, matrix products, on_device(): lax.dot_general(shadow_scaled, coupling, (((1,), (1,)), ((), ())), prefer...  24.1 us
  transfers between devices with their start and end apart: 8, of which 8 were waited for; matrix products, arithmetic and copies ran while one was open for 7% of the time, Pallas kernels for 0%

profile of v1, /device:TPU:1, one launch (start us, length us, event | category | flops | bytes accessed | tf_op | source)
XLA Modules:
  0.0 739.0 jit_solution(13784505021746393224)
XLA Ops:
  7.2 2.0 multiply_convert_fusion.1
  9.3 12.1 %fusion.14 = f32[64,4096]{1,0:T(8,128)} fusion(bf16[4096,2048]{1,0:T(8,128)(2,1)} %param.4, f32[64,2048]{1,0:T(8,128)} %param.7), kind=kOutput, calls=%fused_computation.31 | convolution fusion | flops 1073872896 | bytes 18350080 | tf_op jit(solution)/shard_map/dot_general | solution.py:32
  21.4 29.9 %all-gather.9.cloned.1.call-done = bf16[64,32768]{1,0:T(8,128)(2,1)} async-done(((bf16[64,2048]{1,0:T(8,128)(2,1)}), bf16[64,32768]{1,0:T(8,128)(2,1)}) %all-gather.9.cloned.1.call-update) | async-done | bytes 4194320 | tf_op jit(solution)/shard_map/all_gather | solution.py:26
  51.4 9.8 %fusion.10 = f32[64,2048]{1,0:T(8,128)} fusion(bf16[4096,2048]{1,0:T(8,128)(2,1)} %param.4, bf16[64,32768]{1,0:T(8,128)(2,1)} %all-gather.9.cloned.1.call-done, s32[]{:T(128)S(6)} %select_n.8), kind=kOutput, calls=%fused_computation.24 | convolution fusion | flops 1073741824 | bytes 17825796 | tf_op jit(solution)/shard_map/dot_general | solution.py:28
  61.2 111.6 %all-reduce.4.cloned.1.call-done = f32[64,4096]{1,0:T(8,128)} async-done(((f32[64,4096]{1,0:T(8,128)}), f32[64,4096]{1,0:T(8,128)}) %all-reduce.4.cloned.1.call-update) | async-done | bytes 1048592 | tf_op jit(solution)/shard_map/psum | solution.py:35
  172.9 75.3 %all-gather.17.cloned.1.call-done = f32[512,2048]{1,0:T(8,128)} async-done(((f32[64,2048]{1,0:T(8,128)}), f32[512,2048]{1,0:T(8,128)}) %all-gather.17.cloned.1.call-update) | async-done | bytes 4194320 | tf_op jit(solution)/shard_map/all_gather | solution.py:29
  248.2 2.5 reduce_sum.55
  250.7 0.3 multiply_reduce_fusion.2
  251.0 27.7 %all-reduce = (f32[64]{0:T(128)S(1)}, f32[64]{0:T(128)S(1)}) all-reduce(f32[64]{0:T(128)S(1)} %get-tuple-element.5, f32[64]{0:T(128)S(1)} %get-tuple-element.4), channel_id=1, replica_groups=mesh['row'=8,'col'=16] {'col'}, use_global_device_ids=true, to_apply=%region_1.0 | all-reduce | flops 128 | bytes 1024 | tf_op jit(solution)/shard_map/psum | solution.py:23
  278.7 78.7 %all-gather.11.cloned.1.call-done = f32[64,32768]{1,0:T(8,128)} async-done(((f32[64,4096]{1,0:T(8,128)}), f32[64,32768]{1,0:T(8,128)}) %all-gather.11.cloned.1.call-update) | async-done | bytes 8388624 | tf_op jit(solution)/shard_map/all_gather | solution.py:36
  357.4 1.5 multiply_reduce_fusion.1
  358.9 27.6 %psum.45 = f32[64]{0:T(128)S(1)} all-reduce(f32[64]{0:T(128)S(1)} %get-tuple-element.10), channel_id=1, replica_groups=mesh['row'=8,'col'=16] {'col'}, use_global_device_ids=true, to_apply=%region_7.0 | all-reduce | flops 64 | bytes 512 | tf_op jit(solution)/shard_map/psum | solution.py:51
  386.5 0.9 multiply_convert_fusion
  387.4 12.0 %fusion.12 = f32[64,4096]{1,0:T(8,128)} fusion(bf16[4096,2048]{1,0:T(8,128)(2,1)} %param.4, f32[64,2048]{1,0:T(8,128)S(1)} %get-tuple-element.12, f32[64,2048]{1,0:T(8,128)S(1)} %copy-done, f32[64]{0:T(128)S(1)} %div.10), kind=kOutput, calls=%fused_computation.29 | convolution fusion | flops 1074135040 | bytes 18874624 | tf_op jit(solution)/shard_map/dot_general | solution.py:32
  399.4 0.2 all-gather.19.cloned.1.call-start
  399.7 23.9 %all-gather.13.cloned.1.call-done = bf16[64,32768]{1,0:T(8,128)(2,1)} async-done(((bf16[64,2048]{1,0:T(8,128)(2,1)}), bf16[64,32768]{1,0:T(8,128)(2,1)}) %all-gather.13.cloned.1.call-update) | async-done | bytes 4194320 | tf_op jit(solution)/shard_map/all_gather | solution.py:26
  423.6 9.8 %fusion.8 = f32[64,2048]{1,0:T(8,128)} fusion(bf16[4096,2048]{1,0:T(8,128)(2,1)} %param.4, bf16[64,32768]{1,0:T(8,128)(2,1)} %all-gather.13.cloned.1.call-done, s32[]{:T(128)S(6)} %select_n.8), kind=kOutput, calls=%fused_computation.16 | convolution fusion | flops 1073741824 | bytes 17825796 | tf_op jit(solution)/shard_map/dot_general | solution.py:28
  433.4 111.6 %all-reduce.6.cloned.1.call-done = f32[64,4096]{1,0:T(8,128)} async-done(((f32[64,4096]{1,0:T(8,128)}), f32[64,4096]{1,0:T(8,128)}) %all-reduce.6.cloned.1.call-update) | async-done | bytes 1048592 | tf_op jit(solution)/shard_map/psum | solution.py:35
  545.1 75.1 %all-gather.19.cloned.1.call-done = f32[512,2048]{1,0:T(8,128)} async-done(((f32[64,2048]{1,0:T(8,128)}), f32[512,2048]{1,0:T(8,128)}) %all-gather.19.cloned.1.call-update) | async-done | bytes 4194320 | tf_op jit(solution)/shard_map/all_gather | solution.py:29
  620.2 2.5 reduce_sum.58
  622.6 1.2 multiply_reduce_fusion
  623.8 27.7 %psum.46 = f32[64]{0:T(128)S(1)} all-reduce(f32[64]{0:T(128)S(1)} %get-tuple-element.8), channel_id=1, replica_groups=mesh['row'=8,'col'=16] {'col'}, use_global_device_ids=true, to_apply=%region_10.0 | all-reduce | flops 64 | bytes 512 | tf_op jit(solution)/shard_map/psum | solution.py:43
  651.6 77.7 %all-gather.15.cloned.1.call-done = f32[64,32768]{1,0:T(8,128)} async-done(((f32[64,4096]{1,0:T(8,128)}), f32[64,32768]{1,0:T(8,128)}) %all-gather.15.cloned.1.call-update) | async-done | bytes 8388624 | tf_op jit(solution)/shard_map/all_gather | solution.py:36
  729.3 2.8 multiply_subtract_fusion.4
  (24 shorter events, 0.4 us)
Async XLA Ops:
  7.2 44.2 %all-gather.9.cloned.1.call-start = ((), (), s32[]{:S(2)}) async-start(), calls=%async_computation | async-start | bytes 4456448 | tf_op jit(solution)/shard_map/all_gather | solution.py:26
  9.2 163.6 %all-reduce.4.cloned.1.call-start = ((), (), s32[]{:S(2)}) async-start(), calls=%async_computation.1 | async-start | bytes 2097152 | tf_op jit(solution)/shard_map/psum | solution.py:35
  21.4 229.3 %copy-start = (f32[64,2048]{1,0:T(8,128)S(1)}, f32[64,2048]{1,0:T(8,128)}, u32[]{:S(2)}) copy-start(f32[64,2048]{1,0:T(8,128)} %param.7) | copy-start | bytes 1572868
  21.4 229.3 %copy-start.1 = (f32[64,2048]{1,0:T(8,128)S(1)}, f32[64,2048]{1,0:T(8,128)}, u32[]{:S(2)}) copy-start(f32[64,2048]{1,0:T(8,128)} %param.6) | copy-start | bytes 1572868
  21.4 229.3 %copy-start.2 = (f32[64,2048]{1,0:T(8,128)S(1)}, f32[64,2048]{1,0:T(8,128)}, u32[]{:S(2)}) copy-start(f32[64,2048]{1,0:T(8,128)} %param.5) | copy-start | bytes 1572868
  21.4 226.8 %all-gather.17.cloned.1.call-start = ((), (), s32[]{:S(2)}) async-start(), calls=%async_computation.6 | async-start | bytes 4718592 | tf_op jit(solution)/shard_map/all_gather | solution.py:29
  61.1 296.3 %all-gather.11.cloned.1.call-start = ((), (), s32[]{:S(2)}) async-start(), calls=%async_computation.2 | async-start | bytes 9437184 | tf_op jit(solution)/shard_map/all_gather | solution.py:36
  172.8 250.8 %all-gather.13.cloned.1.call-start = ((), (), s32[]{:S(2)}) async-start(), calls=%async_computation.3 | async-start | bytes 4456448 | tf_op jit(solution)/shard_map/all_gather | solution.py:26
  387.4 157.7 %all-reduce.6.cloned.1.call-start = ((), (), s32[]{:S(2)}) async-start(), calls=%async_computation.4 | async-start | bytes 2097152 | tf_op jit(solution)/shard_map/psum | solution.py:35
  399.4 220.7 %all-gather.19.cloned.1.call-start = ((), (), s32[]{:S(2)}) async-start(), calls=%async_computation.7 | async-start | bytes 4718592 | tf_op jit(solution)/shard_map/all_gather | solution.py:29
  433.4 295.9 %all-gather.15.cloned.1.call-start = ((), (), s32[]{:S(2)}) async-start(), calls=%async_computation.5 | async-start | bytes 9437184 | tf_op jit(solution)/shard_map/all_gather | solution.py:36
Sparse Core Ops, SparseCore 0:
  10.2 41.0 all-gather.8
  53.8 118.9 all-reduce.3
  176.0 72.1 all-gather.16
  250.7 106.7 all-gather.10
  387.5 36.0 all-gather.12
  426.1 118.9 all-reduce.5
  548.0 72.1 all-gather.18
  622.5 106.7 all-gather.14
